TPU v7x, 32 devices: a whole 2x2x4 slice. The times are simulated.
32 devices in a mesh: pipe: 4 (over y, core), seq: 8 (over z, x).
Axes of the slice: x: 2, y: 2, z: 4, core: 2. Of those that a mesh axis runs over, the one named last changes fastest.
Arguments:
- hidden: bfloat16 [2, 192, 3072], P(None, 'seq'), may hold values from -8 to 8
- mod_shift: float32 [4, 3072], P('pipe'), may hold values from -0.3 to 0.3
- mod_scale: float32 [4, 3072], P('pipe'), may hold values from -3 to 3
- mod_gate: float32 [4, 3072], P('pipe'), may hold values from 0.5 to 2.5
- norm_gain: float32 [4, 2, 128], P('pipe'), may hold values from 0.5 to 1.5
- input_proj: bfloat16 [4, 3072, 3, 2048], P('pipe', None, None, 'seq'), may hold values from -0.109375 to 0.109375
- output_proj: bfloat16 [4, 2048, 3072], P('pipe', 'seq'), may hold values from -0.5 to 0.5
- stale_cache: bfloat16 [4, 2, 192, 2, 2048], P('pipe', None, 'seq'), may hold values from -6 to 6
Outputs:
- block_output: bfloat16 [4, 2, 192, 3072], P('pipe', None, 'seq')
- fresh_cache: bfloat16 [4, 2, 192, 2, 2048], P('pipe', None, 'seq')
All inputs are finite; a program needn't handle non-finite values.
Results may differ from a plain program's by a relative error of at most 0.019.
Values may be sent and summed in bfloat16 or wider, within the bound.
No kernel may reach another device: no remote copies, remote signals or barrier semaphores. Data moves between devices by JAX's collectives and lax.ppermute only.
A program may use at most 64 MiB of HBM per device.

v0:
```python
import functools
import math

import jax
import jax.numpy as jnp
from jax import lax
from jax.experimental import pallas as pl
from jax.experimental.pallas import tpu as pltpu
from jax.sharding import PartitionSpec as P

AXES = ("pipe", "seq")
VMEM = pl.BlockSpec(memory_space=pltpu.VMEM)
ANY = pl.BlockSpec(memory_space=pl.ANY)
HBM = pl.BlockSpec(memory_space=pltpu.HBM)


def ring_order(count):
    fast = 1
    while fast * fast * 4 <= count and count % (fast * 2) == 0:
        fast *= 2
    slow = count // fast
    if fast == 1 or slow % 2:
        return list(range(count))
    cells = [(0, 0)]
    for row in range(slow):
        columns = range(1, fast) if row % 2 == 0 else range(fast - 1, 0, -1)
        cells += [(row, column) for column in columns]
    cells += [(row, 0) for row in range(slow - 1, 0, -1)]
    return [row * fast + column for row, column in cells]


def normalise(values, params_ref):
    centered = values - jnp.mean(values, axis=-1, keepdims=True)
    spread = jnp.mean(centered * centered, axis=-1, keepdims=True)
    return (
        centered * lax.rsqrt(spread + 1e-06) * (1.0 + params_ref[1:2, :]) + params_ref[0:1, :]
    ).astype(jnp.bfloat16)


def spread_block(block, buffer, out_ref, sems):
    width = buffer.shape[1]
    buffer[...] = block
    copies = [
        pltpu.make_async_copy(buffer, out_ref.at[shard, :, :width], sems.at[shard])
        for shard in range(out_ref.shape[0])
    ]
    for copy in copies:
        copy.start()
    return copies


def norm_kernel(params_ref, x_ref, out_ref, buffer, sems):
    block = normalise(x_ref[...].astype(jnp.float32), params_ref)
    for copy in spread_block(block, buffer, out_ref, sems):
        copy.wait()


def pack_kernel(params_ref, x_ref, cache_ref, out_ref, buffer, sems, sides, sem):
    count, _, total = sides.shape
    width = x_ref.shape[1]
    channels = total // 2
    block = normalise(x_ref[...].astype(jnp.float32), params_ref)
    copies = spread_block(block, buffer, out_ref, sems)
    for kind in range(2):
        rows = cache_ref[:, kind, :]
        for shard in range(count):
            sides[shard, :, kind * channels : (kind + 1) * channels] = rows[
                :, shard * channels : (shard + 1) * channels
            ]
    copies.append(pltpu.make_async_copy(sides, out_ref.at[:, :, width:], sem))
    copies[-1].start()
    for copy in copies:
        copy.wait()


def attention(head_size, q_ref, kv_ref, far_ref):
    factor = 1.0 / math.sqrt(head_size)
    channels = q_ref.shape[1]
    heads = []
    across = (((1,), (1,)), ((), ()))

    def far_of(kind, start):
        if len(far_ref.shape) == 3:
            return far_ref[kind, :, start : start + head_size]
        return far_ref[:, kind * channels + start : kind * channels + start + head_size]

    for start in range(0, channels, head_size):
        cut = slice(start, start + head_size)
        query = q_ref[:, cut]
        near = lax.dot_general(query, kv_ref[0, :, cut], across, preferred_element_type=jnp.float32)
        far = lax.dot_general(query, far_of(0, start), across, preferred_element_type=jnp.float32)
        near = jnp.exp(near * factor)
        far = jnp.exp(far * factor)
        total = jnp.sum(near, axis=-1, keepdims=True) + jnp.sum(far, axis=-1, keepdims=True)
        near = (near / total).astype(jnp.bfloat16)
        far = (far / total).astype(jnp.bfloat16)
        mixed = jnp.dot(near, kv_ref[1, :, cut], preferred_element_type=jnp.float32)
        mixed = mixed + jnp.dot(far, far_of(1, start), preferred_element_type=jnp.float32)
        heads.append(mixed.astype(jnp.bfloat16))
    return jnp.concatenate(heads, axis=1)


def block_kernel(
    head_size, only, gain_ref, in_ref, out_weights_ref, blocks_ref, far_ref, *refs
):
    caches, refs = refs[:-11], refs[-11:]
    out_ref, kv_ref, blocks, far, w_in, w_out, parts, q_ref, in_sems, sems, part_sems = refs
    width = blocks.shape[1]
    channels = w_out.shape[0]
    pieces = in_sems.shape[1]
    depth = width // pieces
    fetch = pltpu.make_async_copy(blocks_ref.at[:, :width], blocks, sems.at[0])
    fetch.start()
    if len(far.shape) == 3:
        fetch_far = pltpu.make_async_copy(far_ref, far, sems.at[2])
    else:
        begin = far_ref.shape[1] - far.shape[1]
        fetch_far = pltpu.make_async_copy(far_ref.at[:, begin:], far, sems.at[2])
    fetch_far.start()

    for part in (1, 2, 0):
        for piece in range(pieces):
            cut = pl.ds(piece * depth, depth)
            pltpu.make_async_copy(
                in_ref.at[part, cut], w_in.at[part, cut], in_sems.at[part, piece]
            ).start()
    if not only:
        pltpu.make_async_copy(out_weights_ref.at[0], w_out, sems.at[1]).start()
    fetch.wait()
    tokens = blocks[...]
    for part in (1, 2, 0):
        for piece in range(pieces):
            cut = pl.ds(piece * depth, depth)
            pltpu.make_async_copy(
                in_ref.at[part, cut], w_in.at[part, cut], in_sems.at[part, piece]
            ).wait()
        projected = jnp.dot(tokens, w_in[part], preferred_element_type=jnp.float32)
        if part == 2:
            kv_ref[1] = projected.astype(jnp.bfloat16)
            continue
        for start in range(0, channels, head_size):
            head = projected[:, start : start + head_size]
            square = jnp.mean(head * head, axis=-1, keepdims=True)
            head = (head * lax.rsqrt(square + 1e-06) * gain_ref[part : part + 1, :]).astype(
                jnp.bfloat16
            )
            if part == 0:
                q_ref[:, start : start + head_size] = head
            else:
                kv_ref[0, :, start : start + head_size] = head

    fetch_far.wait()
    if only:
        out_ref[:, :channels] = attention(head_size, q_ref, kv_ref, far)
        for patch, cache in enumerate(caches):
            for kind in range(2):
                begin = (1 + 2 * patch + kind) * channels
                out_ref[:, begin : begin + channels] = cache[kind]
        return
    sent = []

    def send(begin, size, sem):
        cut = pl.ds(begin, size)
        sent.append(
            pltpu.make_async_copy(parts.at[:, cut], out_ref.at[:, cut], part_sems.at[sem])
        )
        sent[-1].start()

    steps = part_sems.shape[0]
    attended = attention(head_size, q_ref, kv_ref, far)
    pltpu.make_async_copy(out_weights_ref.at[0], w_out, sems.at[1]).wait()
    tile = width // steps
    for step in range(steps):
        cut = slice(step * tile, (step + 1) * tile)
        update = jnp.dot(attended, w_out[:, cut], preferred_element_type=jnp.float32)
        parts[:, cut] = update.astype(jnp.bfloat16)
        send(step * tile, tile, step)
    for copy in sent:
        copy.wait()


def finish_kernel(params_ref, next_ref, x_ref, parts_ref, out_ref, *rest):
    width = x_ref.shape[1]
    update = jnp.sum(parts_ref[:, :, :width].astype(jnp.float32), axis=0)
    result = (x_ref[...].astype(jnp.float32) + params_ref[2:3, :] * update).astype(jnp.bfloat16)
    out_ref[...] = result
    if rest:
        blocks_ref, buffer, sems = rest
        block = normalise(result.astype(jnp.float32), next_ref)
        for copy in spread_block(block, buffer, blocks_ref, sems):
            copy.wait()


def output_kernel(
    order_ref, params_ref, next_ref, x_ref, att_ref, weights_ref, out_ref, blocks_ref, total, buffer, sems
):
    step = pl.program_id(0)
    channels = weights_ref.shape[0]
    update = jnp.dot(
        att_ref[order_ref[step], :, :channels], weights_ref[...], preferred_element_type=jnp.float32
    )

    @pl.when(step == 0)
    def _():
        total[...] = update

    @pl.when(step > 0)
    def _():
        total[...] += update

    @pl.when(step == pl.num_programs(0) - 1)
    def _():
        result = (x_ref[...].astype(jnp.float32) + params_ref[2:3, :] * total[...]).astype(
            jnp.bfloat16
        )
        out_ref[...] = result
        block = normalise(result.astype(jnp.float32), next_ref)
        for copy in spread_block(block, buffer, blocks_ref, sems):
            copy.wait()


def blank_kernel(*refs):
    pass


def params_of(limit):
    return pltpu.CompilerParams(vmem_limit_bytes=limit << 20)


def body(hidden, mod_shift, mod_scale, mod_gate, norm_gain, input_proj, output_proj, stale_cache):
    sections = lax.axis_size("pipe")
    planes = sections // 2
    seq = lax.axis_size("seq")
    pipe = lax.axis_index("pipe")
    core = lax.rem(pipe, 2)
    plane = pipe // 2
    rows, width = hidden.shape[1:]
    head_size = norm_gain.shape[2]
    channels = input_proj.shape[3]
    tokens = rows * seq
    bf16 = lambda *shape: jax.ShapeDtypeStruct(shape, jnp.bfloat16)

    place = lambda row, position: row * seq + position

    lowest, others = range(2), range(2, sections)

    def swap(value, rows_of=range(sections)):
        pairs = [(place(row, s), place(row ^ 1, s)) for row in rows_of for s in range(seq)]
        return lax.ppermute(value, AXES, pairs)

    def upward(value):
        pairs = [
            (place(row, s), place((row + 2) % sections, s))
            for row in range(sections)
            for s in range(seq)
        ]
        return lax.ppermute(value, AXES, pairs)

    ring = ring_order(seq)

    def around(value, step):
        pairs = [
            (place(row, ring[i]), place(row, ring[(i + step) % seq]))
            for row in others
            for i in range(seq)
        ]
        return lax.ppermute(value, AXES, pairs)

    spot = jnp.array([ring.index(s) for s in range(seq)], jnp.int32)
    half = seq // 2
    moves = [-hop for hop in range(half)] + list(range(1, half)) + [half]
    order = jnp.array(ring, jnp.int32)[
        jnp.remainder(spot[lax.axis_index("seq")] + jnp.array(moves, jnp.int32), seq)
    ]

    def across(blocks):
        return lax.all_to_all(blocks, "seq", split_axis=0, concat_axis=0, tiled=True)

    def blank(*shapes):
        return pl.pallas_call(blank_kernel, out_shape=shapes, out_specs=(ANY,) * len(shapes))()

    gains = jnp.pad(norm_gain[0].reshape(1, -1), ((0, 0), (0, width - 2 * head_size)))
    own_params = jnp.concatenate([mod_shift, mod_scale, mod_gate, gains], axis=0)
    own_in = jnp.transpose(input_proj[0], (1, 0, 2))
    own_out = output_proj
    x = lax.dynamic_index_in_dim(hidden, core, 0, keepdims=False)
    spreading = [pltpu.VMEM((rows, width), jnp.bfloat16), pltpu.SemaphoreType.DMA((seq,))]
    packed = pl.pallas_call(
        pack_kernel, out_shape=bf16(seq, rows, width + 2 * channels),
        in_specs=[VMEM] * 3, out_specs=HBM,
        scratch_shapes=spreading + [
            pltpu.VMEM((seq, rows, 2 * channels), jnp.bfloat16), pltpu.SemaphoreType.DMA,
        ],
        compiler_params=params_of(16),
    )(own_params, x, stale_cache[0, 1])

    other_params = swap(own_params)
    own_in, own_out, other_params, packed = lax.optimization_barrier(
        (own_in, own_out, other_params, packed)
    )
    own = own_in, own_out
    params = [jnp.where(core == turn, own_params, other_params) for turn in range(2)]
    gain_rows = [p[3, : 2 * head_size].reshape(2, head_size) for p in params]
    blocks_shape = bf16(seq, rows, width)

    def norm(x, turn):
        return pl.pallas_call(
            norm_kernel, out_shape=blocks_shape, in_specs=[VMEM] * 2, out_specs=HBM,
            scratch_shapes=spreading, compiler_params=params_of(16),
        )(params[turn], x)

    flat = lambda blocks: blocks.reshape(tokens, blocks.shape[2])
    apart = lambda values: values.reshape(seq, rows, values.shape[1])

    def block(blocks, far, turn, weights, only=False, caches=()):
        total = channels * (1 + 2 * len(caches)) if only else width
        side = (2, tokens, channels) if far.ndim == 3 else (tokens, 2 * channels)
        out, pair = pl.pallas_call(
            functools.partial(block_kernel, head_size, only),
            out_shape=(bf16(tokens, total), pair_shape),
            in_specs=[VMEM] + [HBM] * 2 + [ANY] * 2 + [VMEM] * len(caches),
            out_specs=(VMEM if only else HBM, VMEM),
            scratch_shapes=[
                pltpu.VMEM((tokens, width), jnp.bfloat16),
                pltpu.VMEM(side, jnp.bfloat16),
                pltpu.VMEM(own_in.shape, jnp.bfloat16),
                pltpu.VMEM(own_out.shape[1:], jnp.bfloat16),
                pltpu.VMEM((tokens, width), jnp.bfloat16),
                pltpu.VMEM((tokens, channels), jnp.bfloat16),
                pltpu.SemaphoreType.DMA((3, 2)),
                pltpu.SemaphoreType.DMA((3,)),
                pltpu.SemaphoreType.DMA((4,)),
            ],
            compiler_params=params_of(32),
        )(
            gain_rows[turn], *weights, flat(blocks), far, *caches
        )
        return apart(out), pair

    def output(x, attended, weights, turn):
        return pl.pallas_call(
            output_kernel,
            grid_spec=pltpu.PrefetchScalarGridSpec(
                num_scalar_prefetch=1,
                grid=(seq,),
                in_specs=[
                    pl.BlockSpec((4, width), lambda i, o: (0, 0)),
                    pl.BlockSpec((4, width), lambda i, o: (0, 0)),
                    pl.BlockSpec((rows, width), lambda i, o: (0, 0)),
                    pl.BlockSpec(attended.shape, lambda i, o: (0, 0, 0)),
                    pl.BlockSpec((channels, width), lambda i, o: (i, 0)),
                ],
                out_specs=(pl.BlockSpec((rows, width), lambda i, o: (0, 0)), HBM),
                scratch_shapes=[
                    pltpu.VMEM((rows, width), jnp.float32),
                ] + spreading,
            ),
            out_shape=(bf16(rows, width), blocks_shape),
            compiler_params=params_of(32),
        )(order, params[turn], params[1 - turn], x, attended, weights)

    def finish(x, parts, turn, onward):
        shapes = (bf16(rows, width),) + (blocks_shape,) * onward
        return pl.pallas_call(
            finish_kernel, out_shape=shapes, in_specs=[VMEM] * 4,
            out_specs=(VMEM,) + (HBM,) * onward,
            scratch_shapes=spreading * onward, compiler_params=params_of(16),
        )(params[turn], params[1 - turn], x, parts)

    early = core == 0
    either = lambda on_early, on_late: lax.cond(early, on_early, on_late)

    pair_shape, block_shape = bf16(2, tokens, channels), bf16(rows, width)
    side_shape = bf16(tokens, 2 * channels)
    att_shape = bf16(seq, rows, channels)
    nothing = lambda shape: blank(shape)[0]

    def first_plane():
        other = swap(own_in, lowest), swap(own_out, lowest)

        def start_early():
            received = across(packed)
            parts, fresh = block(received, flat(received), 0, own)
            return parts, fresh, nothing(side_shape)

        def start_late():
            side = flat(across(packed[:, :, width:]))
            return norm(x, 0), nothing(pair_shape), side

        payload, pair0, side = either(start_early, start_late)
        fresh = swap(pair0, lowest)
        received = across(payload)
        side = swap(side, lowest)

        def gather_early():
            result, normed = finish(x, received, 0, 1)
            return normed, nothing(pair_shape), result

        def scatter_late():
            parts, late = block(received, fresh, 0, other)
            return parts, late, nothing(block_shape)

        payload, late_pair, early_x = either(gather_early, scatter_late)
        received = across(payload)

        def scatter_early():
            parts, fresh = block(received, side, 1, other)
            return parts, fresh, nothing(block_shape)

        def gather_late():
            result, normed = finish(x, received, 0, 1)
            return normed, late_pair, result

        payload, pair, late_x = either(scatter_early, gather_late)
        got = swap(pair, lowest)
        received = across(payload)

        def end_early():
            return finish(early_x, received, 1, 0)[0], nothing(pair_shape)

        def end_late():
            parts, late = block(received, got, 1, own)
            return finish(late_x, across(parts), 1, 0)[0], late

        moved, pair1 = either(end_early, end_late)
        return (
            jnp.where(early, early_x, late_x), moved, pair0, got, pair1,
            nothing(side_shape), nothing(side_shape), nothing(bf16(seq * channels, width)), nothing(bf16(*own_in.shape)),
        )

    def other_planes():
        side, mine = lax.optimization_barrier(
            (flat(across(packed[:, :, width:])), own_out[0])
        )
        cut = mine.shape[0] // 2
        streams = [[mine[:cut]], [mine[cut:]], [mine[:cut]], [mine[cut:]]]
        for hop in range(half):
            for stream, step, hops in zip(streams, (1, 1, -1, -1), (half, half - 1, half - 1, half)):
                if hop < hops:
                    stream.append(around(stream[-1], step))
        first, second, third, fourth = streams
        pieces = [piece for pair in zip(first[:half], second) for piece in pair]
        pieces += [piece for pair in zip(third[1:], fourth[1:half]) for piece in pair]
        gathered = jnp.concatenate(pieces + [first[half], fourth[half]], axis=0)
        return (
            nothing(block_shape), nothing(block_shape), nothing(pair_shape), nothing(pair_shape),
            nothing(pair_shape), side, swap(side, others), gathered, swap(own_in, others),
        )

    first_out, moved, pair0, got, pair1, side, other_side, gathered, other_in = lax.cond(
        plane == 0, first_plane, other_planes
    )
    gathered_other = swap(gathered)
    other = other_in, own_out
    first_outs, second_outs = [first_out], [moved]
    firsts = [jnp.where(early, pair0, got)]
    seconds = [jnp.where(early, got, pair1)]
    for level in range(1, planes):
        final = level == planes - 1
        x = upward(moved)
        received = either(lambda: across(norm(x, 0)), lambda: nothing(blocks_shape))

        def attend_early():
            attended, fresh = block(received, side, 0, own, True)
            return across(attended), nothing(blocks_shape), fresh

        def gather_late():
            return nothing(att_shape), across(norm(x, 0)), nothing(pair_shape)

        attended, received, pair0 = either(attend_early, gather_late)
        fresh = swap(pair0)

        def next_early():
            result, normed = output(x, attended, gathered, 0)
            return nothing(att_shape), across(normed), nothing(pair_shape), result

        def attend_late():
            attended, late = block(received, fresh, 0, other, True)
            return across(attended), nothing(blocks_shape), late, nothing(block_shape)

        attended, received, late_pair, early_x = either(next_early, attend_late)

        def attend_again():
            attended, fresh = block(received, other_side, 1, other, True)
            return across(attended), nothing(blocks_shape), fresh, nothing(block_shape)

        def next_late():
            result, normed = output(x, attended, gathered_other, 0)
            return nothing(att_shape), across(normed), late_pair, result

        attended, received, pair, late_x = either(attend_again, next_late)
        got = swap(pair)
        first_outs.append(jnp.where(early, early_x, late_x))
        firsts.append(jnp.where(early, pair0, got))

        def by_plane(values):
            chosen = values[0]
            for at in range(1, level + 1):
                chosen = jnp.where(plane == at, values[at], chosen)
            return chosen

        if final:
            first_cache, second_cache = by_plane(firsts), by_plane(seconds + [got])

        def end_early():
            result, _ = output(early_x, attended, gathered_other, 1)
            if not final:
                return result, nothing(pair_shape)
            caches = jnp.concatenate([*first_cache, *second_cache], axis=1)
            return result, across(apart(caches))

        def end_late():
            if not final:
                attended, late = block(received, got, 1, own, True)
                return output(late_x, across(attended), gathered, 1)[0], late
            attended, late = block(received, got, 1, own, True, (first_cache,))
            late = jnp.where(plane == level, late, second_cache)
            both = jnp.concatenate([flat(attended), *late], axis=1)
            both = across(apart(both))
            return output(late_x, both, gathered, 1)[0], both[:, :, channels:]

        moved, pair1 = either(end_early, end_late)
        second_outs.append(moved)
        seconds.append(jnp.where(early, got, pair1) if not final else None)

    cache = pair1
    mine = by_plane([jnp.where(early, a, b) for a, b in zip(first_outs, second_outs)])
    theirs = swap(by_plane([jnp.where(early, b, a) for a, b in zip(first_outs, second_outs)]))
    block_output = jnp.stack([jnp.where(early, mine, theirs), jnp.where(early, theirs, mine)])
    cache = cache.reshape(seq, rows, 2, 2, channels)
    cache = jnp.transpose(cache, (2, 1, 3, 0, 4)).reshape(2, rows, 2, seq * channels)
    return block_output[None], cache[None]


def solution(mesh):
    in_specs = (
        P(None, "seq", None),
        P("pipe", None),
        P("pipe", None),
        P("pipe", None),
        P("pipe", None, None),
        P("pipe", None, None, "seq"),
        P("pipe", "seq", None),
        P("pipe", None, "seq", None, None),
    )
    out_specs = (P("pipe", None, "seq", None), P("pipe", None, "seq", None, None))
    return jax.shard_map(body, mesh=mesh, in_specs=in_specs, out_specs=out_specs, check_vma=False)
```

profile of v0, /device:TPU:0, one launch (start us, length us, event | category | flops | bytes accessed | tf_op | source)
XLA Modules:
  0.0 309.5 jit_solution(16669727756053374522)
XLA Ops:
  2.0 1.1 slice_bitcast_fusion.cache_ref
  3.1 1.5 shard_map.122
  5.5 132.4 %conditional.10 = (bf16[24,3072]{1,0:T(8,128)(2,1)S(1)}, bf16[24,3072]{1,0:T(8,128)(2,1)}, bf16[2,192,256]{2,1,0:T(8,128)(2,1)S(1)}, bf16[2,192,256]{2,1,0:T(8,1...) conditional(s32[]{:T(128)} %convert_element_type.13, ...), branch_computations={%region_0.1_spmd, %region_1.10_spmd} | conditional | flops 73729 | bytes 92799688 | solution.py:450
  5.6 2.0 collective-permute-start
  7.5 44.4 %conditional = (bf16[8,24,3072]{2,1,0:T(8,128)(2,1)}, bf16[2,192,256]{2,1,0:T(8,128)(2,1)S(1)}, bf16[192,512]{1,0:T(8,128)(2,1)S(1)}) conditional(s32[]{:T(128)} %convert_element_type.2, (f32[4,3072]{1,0:T(4,128)S(1)}, bf16[24,3072]{1,0:T(8,128)(2,1)S(1)}, bf16[8,24,3584]{2,1,0:T(8,128)(2,1)}) %tuple.56, (bf16[8,24,3584]{2,1,0:T(8,128)(2,1)}, ...), branch_computations={%region_2.2_spmd, %region_3.3_spmd} | conditional | bytes 4128824 | solution.py:371
  7.6 7.3 %all-to-all-start.1 = ((bf16[8,24,3584]{2,1,0:T(8,128)(2,1)}), bf16[8,24,3584]{2,1,0:T(8,128)(2,1)S(1)}, u32[]{:S(2)}, u32[]{:S(2)}) async-start(bf16[8,24,3584]{2,1,0:T(8,128)(2,1)} %get-tuple-element.220), calls=%async_computation.1 | async-start | bytes 2752512 | tf_op jit(solution)/shard_map/cond/branch_1_fun/cond/branch_1_fun/all_to_all | solution.py:277
  14.8 30.8 %all-to-all-done.1 = bf16[8,24,3584]{2,1,0:T(8,128)(2,1)S(1)} async-done(((bf16[8,24,3584]{2,1,0:T(8,128)(2,1)}), bf16[8,24,3584]{2,1,0:T(8,128)(2,1)S(1)}, u32[]{:S(2)}, u32[]{:S(2)}) %all-to-all-start.1) | async-done | bytes 1376288 | tf_op jit(solution)/shard_map/cond/branch_1_fun/cond/branch_1_fun/all_to_all | solution.py:277
  45.6 6.3 %branch_1_fun.22 = (bf16[192,3072]{1,0:T(8,128)(2,1)}, bf16[2,192,256]{2,1,0:T(8,128)(2,1)S(1)}) custom-call(f32[2,128]{1,0:T(2,128)S(1)} %get-tuple-element.217.gain_ref, bf16[3,3072,256]{2,1,0:T(8,128)(2,1)} %get-tuple-element.218.in_ref, bf16[1,256,3072]{2,1,0:T(8,128)(2,1)} %get-tuple-element.219.out_weights_ref, bf16[192,3584]{1,0:T(8,128)(2,1)S(1)} %bitcast.47, ...), custom_call_target="tpu_custom_call" | custom-call | tf_op jit(solution)/shard_map/cond/branch_1_fun/cond/branch_1_fun/pallas_call | solution.py:318
  51.9 3.8 %all-to-all-start.10 = ((bf16[8,24,3072]{2,1,0:T(8,128)(2,1)}), bf16[8,24,3072]{2,1,0:T(8,128)(2,1)S(1)}, u32[]{:S(2)}, u32[]{:S(2)}) async-start(bf16[8,24,3072]{2,1,0:T(8,128)(2,1)} %get-tuple-element.271), calls=%async_computation.10 | async-start | bytes 2359296 | tf_op jit(solution)/shard_map/cond/branch_1_fun/all_to_all | solution.py:277
  55.7 1.9 collective-permute-start.1
  57.6 2.4 collective-permute-start.2
  60.0 13.5 %all-to-all-done.10 = bf16[8,24,3072]{2,1,0:T(8,128)(2,1)S(1)} async-done(((bf16[8,24,3072]{2,1,0:T(8,128)(2,1)}), bf16[8,24,3072]{2,1,0:T(8,128)(2,1)S(1)}, u32[]{:S(2)}, u32[]{:S(2)}) %all-to-all-start.10) | async-done | bytes 1179680 | tf_op jit(solution)/shard_map/cond/branch_1_fun/all_to_all | solution.py:277
  73.6 1.6 conditional.1
  73.6 1.6 branch_1_fun.24
  75.9 3.6 %all-to-all-start.11 = ((bf16[8,24,3072]{2,1,0:T(8,128)(2,1)}), bf16[8,24,3072]{2,1,0:T(8,128)(2,1)S(1)}, u32[]{:S(2)}, u32[]{:S(2)}) async-start(bf16[8,24,3072]{2,1,0:T(8,128)(2,1)} %get-tuple-element.275), calls=%async_computation.11 | async-start | bytes 2359296 | tf_op jit(solution)/shard_map/cond/branch_1_fun/all_to_all | solution.py:277
  79.4 1.9 collective-permute-start.3
  81.4 22.5 %all-to-all-done.11 = bf16[8,24,3072]{2,1,0:T(8,128)(2,1)S(1)} async-done(((bf16[8,24,3072]{2,1,0:T(8,128)(2,1)}), bf16[8,24,3072]{2,1,0:T(8,128)(2,1)S(1)}, u32[]{:S(2)}, u32[]{:S(2)}) %all-to-all-start.11) | async-done | bytes 1179680 | tf_op jit(solution)/shard_map/cond/branch_1_fun/all_to_all | solution.py:277
  104.5 7.2 %conditional.2 = (bf16[8,24,3072]{2,1,0:T(8,128)(2,1)}, bf16[2,192,256]{2,1,0:T(8,128)(2,1)}, bf16[24,3072]{1,0:T(8,128)(2,1)S(1)}) conditional(s32[]{:T(128)} %convert_element_type.2, (f32[4,3072]{1,0:T(4,128)S(1)}, f32[4,3072]{1,0:T(4,128)S(1)}, bf16[24,3072]{1,0:T(8,128)(2,1)S(1)}, bf16[8,24,3072]{2,1,0:T(8,128)(2,1)S(1)}, ...), branch_computations={%region_6.6_spmd, %region_7.7_spmd} | conditional | bytes 24 | solution.py:371
  104.5 7.2 %branch_1_fun.26 = (bf16[192,3072]{1,0:T(8,128)(2,1)}, bf16[2,192,256]{2,1,0:T(8,128)(2,1)}) custom-call(f32[2,128]{1,0:T(2,128)S(1)} %get-tuple-element.243.gain_ref, bf16[3,3072,256]{2,1,0:T(8,128)(2,1)} %get-tuple-element.244.in_ref, bf16[1,256,3072]{2,1,0:T(8,128)(2,1)} %get-tuple-element.245.out_weights_ref, bf16[192,3072]{1,0:T(8,128)(2,1)S(1)} %bitcast.59, ...), custom_call_target="tpu_custom_call" | custom-call | tf_op jit(solution)/shard_map/cond/branch_1_fun/cond/branch_1_fun/pallas_call | solution.py:318
  111.8 3.6 %all-to-all-start.12 = ((bf16[8,24,3072]{2,1,0:T(8,128)(2,1)}), bf16[8,24,3072]{2,1,0:T(8,128)(2,1)S(1)}, u32[]{:S(2)}, u32[]{:S(2)}) async-start(bf16[8,24,3072]{2,1,0:T(8,128)(2,1)} %get-tuple-element.280), calls=%async_computation.12 | async-start | bytes 2359296 | tf_op jit(solution)/shard_map/cond/branch_1_fun/all_to_all | solution.py:277
  115.4 2.1 collective-permute-start.4
  117.5 19.6 %all-to-all-done.12 = bf16[8,24,3072]{2,1,0:T(8,128)(2,1)S(1)} async-done(((bf16[8,24,3072]{2,1,0:T(8,128)(2,1)}), bf16[8,24,3072]{2,1,0:T(8,128)(2,1)S(1)}, u32[]{:S(2)}, u32[]{:S(2)}) %all-to-all-start.12) | async-done | bytes 1179680 | tf_op jit(solution)/shard_map/cond/branch_1_fun/all_to_all | solution.py:277
  137.9 23.0 %collective-permute-start.24 = (bf16[2048,3072]{1,0:T(8,128)(2,1)}, bf16[2048,3072]{1,0:T(8,128)(2,1)}, u32[]{:S(2)}, u32[]{:S(2)}) collective-permute-start(bf16[2048,3072]{1,0:T(8,128)(2,1)} %get-tuple-element.389), channel_id=1, source_target_pairs={{0,8},{1,9},{2,10},{3,11},{4,12},{5,13},{6,14},{7,15},{8,0},{9,1},... | collective-permute-start | bytes 37748744 | tf_op jit(solution)/shard_map/ppermute | solution.py:249
  160.9 6.4 %collective-permute-start.22 = (bf16[24,3072]{1,0:T(8,128)(2,1)}, bf16[24,3072]{1,0:T(8,128)(2,1)S(1)}, u32[]{:S(2)}, u32[]{:S(2)}) collective-permute-start(bf16[24,3072]{1,0:T(8,128)(2,1)} %get-tuple-element.383), channel_id=1, source_target_pairs={{0,16},{1,17},{2,18},{3,19},{4,20},{5,21},{6,22},{7,23},{8,24},{9,... | collective-permute-start | bytes 442376 | tf_op jit(solution)/shard_map/ppermute | solution.py:257
  167.9 4.1 %collective-permute-done.22 = bf16[24,3072]{1,0:T(8,128)(2,1)S(1)} collective-permute-done((bf16[24,3072]{1,0:T(8,128)(2,1)}, bf16[24,3072]{1,0:T(8,128)(2,1)S(1)}, u32[]{:S(2)}, u32[]{:S(2)}) %collective-permute-start.22) | collective-permute-done | bytes 147488 | tf_op jit(solution)/shard_map/ppermute | solution.py:257
  172.0 34.0 %conditional.11 = (bf16[8,24,3072]{2,1,0:T(8,128)(2,1)S(1)}) conditional(s32[]{:T(128)} %convert_element_type.12, () %tuple.92, (f32[4,3072]{1,0:T(4,128)S(1)}, bf16[24,3072]{1,0:T(8,128)(2,1)S(1)}) %tuple.91), branch_computations={%region_10.11_spmd, %region_11.12_spmd} | conditional | bytes 2359304 | solution.py:371
  172.0 1.9 branch_1_fun.34
  173.9 32.1 %all_to_all.66 = bf16[8,24,3072]{2,1,0:T(8,128)(2,1)S(1)} all-to-all(bf16[8,24,3072]{2,1,0:T(8,128)(2,1)S(1)} %branch_1_fun.34), channel_id=1, replica_groups=mesh['pipe'=4,'seq'=8] {'seq'}, dimensions={0} | all-to-all | bytes 2359296 | tf_op jit(solution)/shard_map/cond/branch_1_fun/all_to_all | solution.py:277
  206.0 16.8 %conditional.12 = (bf16[8,24,256]{2,1,0:T(8,128)(2,1)}, bf16[8,24,3072]{2,1,0:T(8,128)(2,1)S(1)}, bf16[2,192,256]{2,1,0:T(8,128)(2,1)S(1)}) conditional(s32[]{:T(128)} %convert_element_type.12, (f32[4,3072]{1,0:T(4,128)S(1)}, bf16[24,3072]{1,0:T(8,128)(2,1)S(1)}) %tuple.91, (bf16[8,24,3072]{2,1,0:T(8,128)(2,1)S(1)}, f32[2,128]{1,0:T(2,128)S(1)}, ...), branch_computations={%region_12.13_spmd, %region_13.14_spmd} | conditional | bytes 3539000 | solution.py:371
  206.0 5.6 %branch_1_fun.35 = (bf16[192,256]{1,0:T(8,128)(2,1)}, bf16[2,192,256]{2,1,0:T(8,128)(2,1)S(1)}) custom-call(f32[2,128]{1,0:T(2,128)S(1)} %get-tuple-element.288.gain_ref, bf16[3,3072,256]{2,1,0:T(8,128)(2,1)} %get-tuple-element.289.in_ref, bf16[1,256,3072]{2,1,0:T(8,128)(2,1)} %get-tuple-element.290.out_weights_ref, bf16[192,3072]{1,0:T(8,128)(2,1)S(1)} %bitcast.62, ...), custom_call_target="tpu_custom_call" | custom-call | tf_op jit(solution)/shard_map/cond/branch_1_fun/pallas_call | solution.py:318
  211.6 4.0 %all-to-all-start.5 = ((bf16[8,24,256]{2,1,0:T(8,128)(2,1)}), bf16[8,24,256]{2,1,0:T(8,128)(2,1)}, u32[]{:S(2)}, u32[]{:S(2)}) async-start(bf16[8,24,256]{2,1,0:T(8,128)(2,1)} %bitcast.12), calls=%async_computation.5 | async-start | bytes 196608 | tf_op jit(solution)/shard_map/cond/branch_1_fun/all_to_all | solution.py:277
  215.6 7.1 %all-to-all-done.5 = bf16[8,24,256]{2,1,0:T(8,128)(2,1)} async-done(((bf16[8,24,256]{2,1,0:T(8,128)(2,1)}), bf16[8,24,256]{2,1,0:T(8,128)(2,1)}, u32[]{:S(2)}, u32[]{:S(2)}) %all-to-all-start.5) | async-done | bytes 98336 | tf_op jit(solution)/shard_map/cond/branch_1_fun/all_to_all | solution.py:277
  224.2 32.2 %conditional.13 = (bf16[8,24,256]{2,1,0:T(8,128)(2,1)S(1)}, bf16[8,24,3072]{2,1,0:T(8,128)(2,1)}, bf16[2,192,256]{2,1,0:T(8,128)(2,1)S(1)}, bf16[24,3072]{1,0:T(8,128)(2,1)S(1)}) conditional(s32[]{:T(128)} %convert_element_type.12, (bf16[8,24,3072]{2,1,0:T(8,128)(2,1)S(1)}, f32[2,128]{1,0:T(2,128)S(1)}, bf16[3,3072,256]{2,1,0:T(8,128)(2,1)}, ...), branch_computations={%region_14.15_spmd, %region_15.16_spmd} | conditional | bytes 3539008 | solution.py:371
  224.2 10.1 %branch_1_fun.38 = (bf16[24,3072]{1,0:T(8,128)(2,1)S(1)}, bf16[8,24,3072]{2,1,0:T(8,128)(2,1)}) custom-call(s32[8]{0:T(128)S(1)} %get-tuple-element.302.order_ref, f32[4,3072]{1,0:T(4,128)S(1)} %get-tuple-element.303.params_ref, f32[4,3072]{1,0:T(4,128)S(1)} %get-tuple-element.304.next_ref, bf16[24,3072]{1,0:T(8,128)(2,1)S(1)} %get-tuple-element.305.x_ref, ...), custom_call_target="tpu_custom_call" | custom-call | tf_op jit(solution)/shard_map/cond/branch_1_fun/pallas_call | solution.py:341
  234.3 4.2 %all-to-all-start.7 = ((bf16[8,24,3072]{2,1,0:T(8,128)(2,1)}), bf16[8,24,3072]{2,1,0:T(8,128)(2,1)}, u32[]{:S(2)}, u32[]{:S(2)}) async-start(bf16[8,24,3072]{2,1,0:T(8,128)(2,1)} %get-tuple-element.308), calls=%async_computation.7 | async-start | bytes 2359296 | tf_op jit(solution)/shard_map/cond/branch_1_fun/all_to_all | solution.py:277
  238.6 17.8 %all-to-all-done.7 = bf16[8,24,3072]{2,1,0:T(8,128)(2,1)} async-done(((bf16[8,24,3072]{2,1,0:T(8,128)(2,1)}), bf16[8,24,3072]{2,1,0:T(8,128)(2,1)}, u32[]{:S(2)}, u32[]{:S(2)}) %all-to-all-start.7) | async-done | bytes 1179680 | tf_op jit(solution)/shard_map/cond/branch_1_fun/all_to_all | solution.py:277
  256.4 17.5 %conditional.14 = (bf16[8,24,256]{2,1,0:T(8,128)(2,1)}, bf16[8,24,3072]{2,1,0:T(8,128)(2,1)S(1)}, bf16[2,192,256]{2,1,0:T(8,128)(2,1)S(1)}, bf16[24,3072]{1,0:T(8,128)(2,1)S(1)}) conditional(s32[]{:T(128)} %convert_element_type.12, (s32[8]{0:T(128)S(1)}, f32[4,3072]{1,0:T(4,128)S(1)}, f32[4,3072]{1,0:T(4,128)S(1)}, ...), branch_computations={%region_16.17_spmd, %region_17.18_spmd} | conditional | bytes 3539008 | solution.py:371
  256.4 6.3 %branch_1_fun.40 = (bf16[192,256]{1,0:T(8,128)(2,1)}, bf16[2,192,256]{2,1,0:T(8,128)(2,1)S(1)}) custom-call(f32[2,128]{1,0:T(2,128)S(1)} %get-tuple-element.319.gain_ref, bf16[3,3072,256]{2,1,0:T(8,128)(2,1)} %get-tuple-element.320.in_ref, bf16[1,256,3072]{2,1,0:T(8,128)(2,1)} %get-tuple-element.321.out_weights_ref, bf16[192,3072]{1,0:T(8,128)(2,1)} %bitcast.15.blocks_ref, ...), custom_call_target="tpu_custom_call" | custom-call | tf_op jit(solution)/shard_map/cond/branch_1_fun/pallas_call | solution.py:318
  262.7 4.0 %all-to-all-start.9 = ((bf16[8,24,256]{2,1,0:T(8,128)(2,1)}), bf16[8,24,256]{2,1,0:T(8,128)(2,1)}, u32[]{:S(2)}, u32[]{:S(2)}) async-start(bf16[8,24,256]{2,1,0:T(8,128)(2,1)} %bitcast.16), calls=%async_computation.9 | async-start | bytes 196608 | tf_op jit(solution)/shard_map/cond/branch_1_fun/all_to_all | solution.py:277
  266.8 7.1 %all-to-all-done.9 = bf16[8,24,256]{2,1,0:T(8,128)(2,1)} async-done(((bf16[8,24,256]{2,1,0:T(8,128)(2,1)}), bf16[8,24,256]{2,1,0:T(8,128)(2,1)}, u32[]{:S(2)}, u32[]{:S(2)}) %all-to-all-start.9) | async-done | bytes 98336 | tf_op jit(solution)/shard_map/cond/branch_1_fun/all_to_all | solution.py:277
  273.9 1.4 collective-permute-done.25
  275.3 1.0 select_select_fusion
  276.3 15.1 %conditional.15 = (bf16[24,3072]{1,0:T(8,128)(2,1)S(1)}, bf16[8,24,1024]{2,1,0:T(8,128)(2,1)}) conditional(s32[]{:T(128)} %convert_element_type.12, (bf16[8,24,3072]{2,1,0:T(8,128)(2,1)S(1)}, f32[2,128]{1,0:T(2,128)S(1)}, bf16[3,3072,256]{2,1,0:T(8,128)(2,1)}, bf16[1,256,3072]{2,1,0:T(8,128)(2,1)}, bf16[2,192,256]{2,1,0:T(8,128)(2,1)S(1)}, ...), branch_computations={%region_18.19_spmd, %region_19.20_spmd} | conditional | flops 1572865 | bytes 3735578 | solution.py:371
  277.2 4.1 %all-to-all-start.15 = ((bf16[8,24,1024]{2,1,0:T(8,128)(2,1)}), bf16[8,24,1024]{2,1,0:T(8,128)(2,1)}, u32[]{:S(2)}, u32[]{:S(2)}) async-start(bf16[8,24,1024]{2,1,0:T(8,128)(2,1)} %pad_maximum_fusion.1), calls=%async_computation.15 | async-start | bytes 786432 | tf_op jit(solution)/shard_map/cond/branch_1_fun/all_to_all | solution.py:277
  281.3 10.1 %branch_1_fun.43 = (bf16[24,3072]{1,0:T(8,128)(2,1)S(1)}, bf16[8,24,3072]{2,1,0:T(8,128)(2,1)}) custom-call(s32[8]{0:T(128)S(1)} %get-tuple-element.342.order_ref, f32[4,3072]{1,0:T(4,128)S(1)} %get-tuple-element.343.params_ref, f32[4,3072]{1,0:T(4,128)S(1)} %get-tuple-element.344.next_ref, bf16[24,3072]{1,0:T(8,128)(2,1)S(1)} %get-tuple-element.345.x_ref, ...), custom_call_target="tpu_custom_call" | custom-call | tf_op jit(solution)/shard_map/cond/branch_1_fun/pallas_call | solution.py:341
  291.4 1.0 select_select_fusion.2
  292.4 13.7 %collective-permute-start.26 = (bf16[24,3072]{1,0:T(8,128)(2,1)S(1)}, bf16[24,3072]{1,0:T(8,128)(2,1)S(1)}, u32[]{:S(2)}, u32[]{:S(2)}) collective-permute-start(bf16[24,3072]{1,0:T(8,128)(2,1)S(1)} %select_select_fusion.2), channel_id=1, source_target_pairs={{0,8},{1,9},{2,10},{3,11},{4,12},{5,13},{6,14},{7,15},{8,0},{9,1},... | collective-permute-start | bytes 442376 | tf_op jit(solution)/shard_map/ppermute | solution.py:249
  306.1 1.3 reshape.74
  (65 shorter events, 10.3 us)
Async XLA Ops:
  0.6 2.5 copy-start
  1.5 3.2 %collective-permute-start.21 = (f32[4,3072]{1,0:T(4,128)S(1)}, f32[4,3072]{1,0:T(4,128)S(1)}, u32[]{:S(2)}, u32[]{:S(2)}) collective-permute-start(f32[4,3072]{1,0:T(4,128)S(1)} %select_maximum_fusion.params_ref), channel_id=1, source_target_pairs={{0,8},{1,9},{2,10},{3,11},{4,12},{5,13},{6,14},{7,15},{8,0},{9,1},... | collective-permute-start | bytes 147464 | tf_op jit(solution)/shard_map/ppermute | solution.py:249
  5.5 161.8 %copy-start.9 = (s32[8]{0:T(128)S(1)}, s32[8]{0:T(128)}, u32[]{:S(2)}) copy-start(s32[8]{0:T(128)} %constant.55.clone) | copy-start | bytes 100
  5.6 68.0 %collective-permute-start = (bf16[3,3072,256]{2,1,0:T(8,128)(2,1)}, bf16[3,3072,256]{2,1,0:T(8,128)(2,1)}, u32[]{:S(2)}, u32[]{:S(2)}) collective-permute-start(bf16[3,3072,256]{2,1,0:T(8,128)(2,1)} %get-tuple-element.269), channel_id=1, source_target_pairs={{0,8},{1,9},{2,10},{3,11},{4,12},{5,13},{6,14},{7,15},{8,0},{9,1},... | collective-permute-start | bytes 14155784 | tf_op jit(solution)/shard_map/cond/branch_1_fun/ppermute | solution.py:249
  7.6 38.1 %all-to-all-start.1 = ((bf16[8,24,3584]{2,1,0:T(8,128)(2,1)}), bf16[8,24,3584]{2,1,0:T(8,128)(2,1)S(1)}, u32[]{:S(2)}, u32[]{:S(2)}) async-start(bf16[8,24,3584]{2,1,0:T(8,128)(2,1)} %get-tuple-element.220), calls=%async_computation.1 | async-start | bytes 2752512 | tf_op jit(solution)/shard_map/cond/branch_1_fun/cond/branch_1_fun/all_to_all | solution.py:277
  51.9 59.9 %copy-start.4 = (bf16[2,192,256]{2,1,0:T(8,128)(2,1)}, bf16[2,192,256]{2,1,0:T(8,128)(2,1)S(1)}, u32[]{:S(2)}) copy-start(bf16[2,192,256]{2,1,0:T(8,128)(2,1)S(1)} %get-tuple-element.454) | copy-start | bytes 589828 | tf_op jit(solution)/shard_map/cond
  51.9 21.6 %all-to-all-start.10 = ((bf16[8,24,3072]{2,1,0:T(8,128)(2,1)}), bf16[8,24,3072]{2,1,0:T(8,128)(2,1)S(1)}, u32[]{:S(2)}, u32[]{:S(2)}) async-start(bf16[8,24,3072]{2,1,0:T(8,128)(2,1)} %get-tuple-element.271), calls=%async_computation.10 | async-start | bytes 2359296 | tf_op jit(solution)/shard_map/cond/branch_1_fun/all_to_all | solution.py:277
  55.7 17.9 %collective-permute-start.1 = (bf16[1,256,3072]{2,1,0:T(8,128)(2,1)}, bf16[1,256,3072]{2,1,0:T(8,128)(2,1)}, u32[]{:S(2)}, u32[]{:S(2)}) collective-permute-start(bf16[1,256,3072]{2,1,0:T(8,128)(2,1)} %get-tuple-element.270), channel_id=1, source_target_pairs={{0,8},{1,9},{2,10},{3,11},{4,12},{5,13},{6,14},{7,15},{8,0},{9,1},... | collective-permute-start | bytes 4718600 | tf_op jit(solution)/shard_map/cond/branch_1_fun/ppermute | solution.py:249
  57.6 15.9 %collective-permute-start.2 = (bf16[2,192,256]{2,1,0:T(8,128)(2,1)S(1)}, bf16[2,192,256]{2,1,0:T(8,128)(2,1)S(1)}, u32[]{:S(2)}, u32[]{:S(2)}) collective-permute-start(bf16[2,192,256]{2,1,0:T(8,128)(2,1)S(1)} %get-tuple-element.454), channel_id=1, source_target_pairs={{0,8},{1,9},{2,10},{3,11},{4,12},{5,13},{6,14},{7,15},{8,0},{9,1},... | collective-permute-start | bytes 589832 | tf_op jit(solution)/shard_map/cond/branch_1_fun/ppermute | solution.py:249
  75.2 0.7 copy-start.7
  75.9 28.0 %all-to-all-start.11 = ((bf16[8,24,3072]{2,1,0:T(8,128)(2,1)}), bf16[8,24,3072]{2,1,0:T(8,128)(2,1)S(1)}, u32[]{:S(2)}, u32[]{:S(2)}) async-start(bf16[8,24,3072]{2,1,0:T(8,128)(2,1)} %get-tuple-element.275), calls=%async_computation.11 | async-start | bytes 2359296 | tf_op jit(solution)/shard_map/cond/branch_1_fun/all_to_all | solution.py:277
  79.4 24.4 %collective-permute-start.3 = (bf16[192,512]{1,0:T(8,128)(2,1)S(1)}, bf16[192,512]{1,0:T(8,128)(2,1)S(1)}, u32[]{:S(2)}, u32[]{:S(2)}) collective-permute-start(bf16[192,512]{1,0:T(8,128)(2,1)S(1)} %get-tuple-element.278), channel_id=1, source_target_pairs={{0,8},{1,9},{2,10},{3,11},{4,12},{5,13},{6,14},{7,15},{8,0},{9,1},... | collective-permute-start | bytes 589832 | tf_op jit(solution)/shard_map/cond/branch_1_fun/ppermute | solution.py:249
  103.8 0.7 copy-start.6
  104.5 32.5 %copy-start.3 = (bf16[1,256,3072]{2,1,0:T(8,128)(2,1)S(1)}, bf16[1,256,3072]{2,1,0:T(8,128)(2,1)}, u32[]{:S(2)}) copy-start(bf16[1,256,3072]{2,1,0:T(8,128)(2,1)} %get-tuple-element.270) | copy-start | bytes 4718596 | tf_op jit(solution)/shard_map/cond
  111.8 25.3 %all-to-all-start.12 = ((bf16[8,24,3072]{2,1,0:T(8,128)(2,1)}), bf16[8,24,3072]{2,1,0:T(8,128)(2,1)S(1)}, u32[]{:S(2)}, u32[]{:S(2)}) async-start(bf16[8,24,3072]{2,1,0:T(8,128)(2,1)} %get-tuple-element.280), calls=%async_computation.12 | async-start | bytes 2359296 | tf_op jit(solution)/shard_map/cond/branch_1_fun/all_to_all | solution.py:277
  115.4 22.5 %copy-start.5 = (bf16[2,192,256]{2,1,0:T(8,128)(2,1)S(1)}, bf16[2,192,256]{2,1,0:T(8,128)(2,1)}, u32[]{:S(2)}) copy-start(bf16[2,192,256]{2,1,0:T(8,128)(2,1)} %copy-done.4) | copy-start | bytes 589828 | tf_op jit(solution)/shard_map/cond
  115.4 21.6 %collective-permute-start.4 = (bf16[2,192,256]{2,1,0:T(8,128)(2,1)}, bf16[2,192,256]{2,1,0:T(8,128)(2,1)}, u32[]{:S(2)}, u32[]{:S(2)}) collective-permute-start(bf16[2,192,256]{2,1,0:T(8,128)(2,1)} %get-tuple-element.281), channel_id=1, source_target_pairs={{0,8},{1,9},{2,10},{3,11},{4,12},{5,13},{6,14},{7,15},{8,0},{9,1},... | collective-permute-start | bytes 589832 | tf_op jit(solution)/shard_map/cond/branch_1_fun/ppermute | solution.py:249
  137.9 84.9 %copy-start.8 = (s32[8]{0:T(128)S(1)}, s32[8]{0:T(128)}, u32[]{:S(2)}) copy-start(s32[8]{0:T(128)} %constant.57.clone) | copy-start | bytes 100
  137.9 85.5 %copy-start.2 = (s32[8]{0:T(128)S(1)}, s32[8]{0:T(128)}, u32[]{:S(2)}) copy-start(s32[8]{0:T(128)} %constant.56.clone) | copy-start | bytes 100
  137.9 118.5 %collective-permute-start.24 = (bf16[2048,3072]{1,0:T(8,128)(2,1)}, bf16[2048,3072]{1,0:T(8,128)(2,1)}, u32[]{:S(2)}, u32[]{:S(2)}) collective-permute-start(bf16[2048,3072]{1,0:T(8,128)(2,1)} %get-tuple-element.389), channel_id=1, source_target_pairs={{0,8},{1,9},{2,10},{3,11},{4,12},{5,13},{6,14},{7,15},{8,0},{9,1},... | collective-permute-start | bytes 37748744 | tf_op jit(solution)/shard_map/ppermute | solution.py:249
  160.9 11.1 %collective-permute-start.22 = (bf16[24,3072]{1,0:T(8,128)(2,1)}, bf16[24,3072]{1,0:T(8,128)(2,1)S(1)}, u32[]{:S(2)}, u32[]{:S(2)}) collective-permute-start(bf16[24,3072]{1,0:T(8,128)(2,1)} %get-tuple-element.383), channel_id=1, source_target_pairs={{0,16},{1,17},{2,18},{3,19},{4,20},{5,21},{6,22},{7,23},{8,24},{9,... | collective-permute-start | bytes 442376 | tf_op jit(solution)/shard_map/ppermute | solution.py:257
  211.6 11.1 %all-to-all-start.5 = ((bf16[8,24,256]{2,1,0:T(8,128)(2,1)}), bf16[8,24,256]{2,1,0:T(8,128)(2,1)}, u32[]{:S(2)}, u32[]{:S(2)}) async-start(bf16[8,24,256]{2,1,0:T(8,128)(2,1)} %bitcast.12), calls=%async_computation.5 | async-start | bytes 196608 | tf_op jit(solution)/shard_map/cond/branch_1_fun/all_to_all | solution.py:277
  222.8 1.4 collective-permute-start.23
  234.3 22.1 %all-to-all-start.7 = ((bf16[8,24,3072]{2,1,0:T(8,128)(2,1)}), bf16[8,24,3072]{2,1,0:T(8,128)(2,1)}, u32[]{:S(2)}, u32[]{:S(2)}) async-start(bf16[8,24,3072]{2,1,0:T(8,128)(2,1)} %get-tuple-element.308), calls=%async_computation.7 | async-start | bytes 2359296 | tf_op jit(solution)/shard_map/cond/branch_1_fun/all_to_all | solution.py:277
  262.7 11.1 %all-to-all-start.9 = ((bf16[8,24,256]{2,1,0:T(8,128)(2,1)}), bf16[8,24,256]{2,1,0:T(8,128)(2,1)}, u32[]{:S(2)}, u32[]{:S(2)}) async-start(bf16[8,24,256]{2,1,0:T(8,128)(2,1)} %bitcast.16), calls=%async_computation.9 | async-start | bytes 196608 | tf_op jit(solution)/shard_map/cond/branch_1_fun/all_to_all | solution.py:277
  273.9 1.4 collective-permute-start.25
  277.2 14.2 %all-to-all-start.15 = ((bf16[8,24,1024]{2,1,0:T(8,128)(2,1)}), bf16[8,24,1024]{2,1,0:T(8,128)(2,1)}, u32[]{:S(2)}, u32[]{:S(2)}) async-start(bf16[8,24,1024]{2,1,0:T(8,128)(2,1)} %pad_maximum_fusion.1), calls=%async_computation.15 | async-start | bytes 786432 | tf_op jit(solution)/shard_map/cond/branch_1_fun/all_to_all | solution.py:277
  291.4 18.1 %copy-start.1 = (bf16[2,24,3072]{2,1,0:T(8,128)(2,1)S(1)}, bf16[2,24,3072]{2,1,0:T(8,128)(2,1)}, u32[]{:S(2)}) copy-start(bf16[2,24,3072]{2,1,0:T(8,128)(2,1)} %param.31) | copy-start | bytes 884740
  292.4 16.3 %collective-permute-start.26 = (bf16[24,3072]{1,0:T(8,128)(2,1)S(1)}, bf16[24,3072]{1,0:T(8,128)(2,1)S(1)}, u32[]{:S(2)}, u32[]{:S(2)}) collective-permute-start(bf16[24,3072]{1,0:T(8,128)(2,1)S(1)} %select_select_fusion.2), channel_id=1, source_target_pairs={{0,8},{1,9},{2,10},{3,11},{4,12},{5,13},{6,14},{7,15},{8,0},{9,1},... | collective-permute-start | bytes 442376 | tf_op jit(solution)/shard_map/ppermute | solution.py:249
where the time goes:
time: 311 us; the launch traced here: 310 us
  waiting for transfers between devices  124 us (40%)
  starting transfers between devices  88.4 us (28%)
  Pallas kernels  51.5 us (17%)
  blocking collectives  32.1 us (10%)
  local copies, waits for them, and re-layouts  6.29 us (2%)
  other arithmetic  5.9 us (2%)
    all_to_all x8, waiting for transfers between devices, across(): lax.all_to_all(blocks, 'seq', split_axis=0, concat_axis=0, tiled=True)  118 us
    ppermute x10, starting transfers between devices, swap(): return lax.ppermute(value, AXES, pairs)  47.5 us
    all_to_all x8, starting transfers between devices, across(): lax.all_to_all(blocks, 'seq', split_axis=0, concat_axis=0, tiled=True)  34.5 us
    all_to_all x1, blocking collectives, across(): lax.all_to_all(blocks, 'seq', split_axis=0, concat_axis=0, tiled=True)  32.1 us
    pallas_call x4, Pallas kernels, block(): pl.pallas_call(functools.partial(block_kernel, head_size, only), out_shap...  25.4 us
    pallas_call x2, Pallas kernels, output(): pl.pallas_call(output_kernel, grid_spec=pltpu.PrefetchScalarGridSpec(num_...  20.2 us
    ppermute x1, starting transfers between devices, upward(): return lax.ppermute(value, AXES, pairs)  6.42 us
  transfers between devices with their start and end apart: 19, of which 10 were waited for; matrix products, arithmetic and copies ran while one was open for 2% of the time, Pallas kernels for 11%

commit v1 on v0

--- a/solution.py
+++ b/solution.py
@@ -192,8 +192,9 @@
 
 
 def output_kernel(
-    order_ref, params_ref, next_ref, x_ref, att_ref, weights_ref, out_ref, blocks_ref, total, buffer, sems
+    order_ref, params_ref, next_ref, x_ref, att_ref, weights_ref, out_ref, *rest
 ):
+    total, rest = rest[-1], rest[:-1]
     step = pl.program_id(0)
     channels = weights_ref.shape[0]
     update = jnp.dot(
@@ -214,9 +215,11 @@
             jnp.bfloat16
         )
         out_ref[...] = result
-        block = normalise(result.astype(jnp.float32), next_ref)
-        for copy in spread_block(block, buffer, blocks_ref, sems):
-            copy.wait()
+        if rest:
+            blocks_ref, buffer, sems = rest
+            block = normalise(result.astype(jnp.float32), next_ref)
+            for copy in spread_block(block, buffer, blocks_ref, sems):
+                copy.wait()
 
 
 def blank_kernel(*refs):
@@ -337,7 +340,7 @@
         )
         return apart(out), pair
 
-    def output(x, attended, weights, turn):
+    def output(x, attended, weights, turn, onward=False):
         return pl.pallas_call(
             output_kernel,
             grid_spec=pltpu.PrefetchScalarGridSpec(
@@ -350,12 +353,10 @@
                     pl.BlockSpec(attended.shape, lambda i, o: (0, 0, 0)),
                     pl.BlockSpec((channels, width), lambda i, o: (i, 0)),
                 ],
-                out_specs=(pl.BlockSpec((rows, width), lambda i, o: (0, 0)), HBM),
-                scratch_shapes=[
-                    pltpu.VMEM((rows, width), jnp.float32),
-                ] + spreading,
+                out_specs=(pl.BlockSpec((rows, width), lambda i, o: (0, 0)),) + (HBM,) * onward,
+                scratch_shapes=spreading * onward + [pltpu.VMEM((rows, width), jnp.float32)],
             ),
-            out_shape=(bf16(rows, width), blocks_shape),
+            out_shape=(bf16(rows, width),) + (blocks_shape,) * onward,
             compiler_params=params_of(32),
         )(order, params[turn], params[1 - turn], x, attended, weights)
 
@@ -389,6 +390,7 @@
 
         payload, pair0, side = either(start_early, start_late)
         fresh = swap(pair0, lowest)
+        fresh, side = lax.optimization_barrier((fresh, side))
         received = across(payload)
         side = swap(side, lowest)
 
@@ -434,10 +436,15 @@
         )
         cut = mine.shape[0] // 2
         streams = [[mine[:cut]], [mine[cut:]], [mine[:cut]], [mine[cut:]]]
+        def advance(one, two):
+            ahead, behind = lax.optimization_barrier((streams[one][-1], streams[two][-1]))
+            streams[one].append(around(ahead, 1))
+            streams[two].append(around(behind, -1))
+
         for hop in range(half):
-            for stream, step, hops in zip(streams, (1, 1, -1, -1), (half, half - 1, half - 1, half)):
-                if hop < hops:
-                    stream.append(around(stream[-1], step))
+            advance(0, 3)
+            if hop < half - 1:
+                advance(1, 2)
         first, second, third, fourth = streams
         pieces = [piece for pair in zip(first[:half], second) for piece in pair]
         pieces += [piece for pair in zip(third[1:], fourth[1:half]) for piece in pair]
@@ -471,7 +478,7 @@
         fresh = swap(pair0)
 
         def next_early():
-            result, normed = output(x, attended, gathered, 0)
+            result, normed = output(x, attended, gathered, 0, True)
             return nothing(att_shape), across(normed), nothing(pair_shape), result
 
         def attend_late():
@@ -485,7 +492,7 @@
             return across(attended), nothing(blocks_shape), fresh, nothing(block_shape)
 
         def next_late():
-            result, normed = output(x, attended, gathered_other, 0)
+            result, normed = output(x, attended, gathered_other, 0, True)
             return nothing(att_shape), across(normed), late_pair, result
 
         attended, received, pair, late_x = either(attend_again, next_late)
@@ -503,7 +510,7 @@
             first_cache, second_cache = by_plane(firsts), by_plane(seconds + [got])
 
         def end_early():
-            result, _ = output(early_x, attended, gathered_other, 1)
+            result = output(early_x, attended, gathered_other, 1)[0]
             if not final:
                 return result, nothing(pair_shape)
             caches = jnp.concatenate([*first_cache, *second_cache], axis=1)

time: 311 us -> 305 us (0.981)
  starting transfers between devices: 88.4 us -> 81.3 us
    ppermute x1, starting transfers between devices: 6.42 us -> 0.01 us  [upward(): return lax.ppermute(value, AXES, pairs)]
  transfers between devices with their start and end apart: 19 -> 19, of which waited for: 10 -> 12; matrix products, arithmetic and copies ran while one was open for 2% -> 2% of each run, Pallas kernels for 11% -> 11%
where the time goes in v1:
time: 305 us; the launch traced here: 303 us
  waiting for transfers between devices  126 us (41%)
  starting transfers between devices  81.3 us (27%)
  Pallas kernels  50.1 us (16%)
  blocking collectives  31.6 us (10%)
  local copies, waits for them, and re-layouts  6.29 us (2%)
  other arithmetic  5.88 us (2%)
    all_to_all x8, waiting for transfers between devices, across(): lax.all_to_all(blocks, 'seq', split_axis=0, concat_axis=0, tiled=True)  118 us
    ppermute x10, starting transfers between devices, swap(): return lax.ppermute(value, AXES, pairs)  46.7 us
    all_to_all x8, starting transfers between devices, across(): lax.all_to_all(blocks, 'seq', split_axis=0, concat_axis=0, tiled=True)  34.6 us
    all_to_all x1, blocking collectives, across(): lax.all_to_all(blocks, 'seq', split_axis=0, concat_axis=0, tiled=True)  31.6 us
    pallas_call x4, Pallas kernels, block(): pl.pallas_call(functools.partial(block_kernel, head_size, only), out_shap...  25.4 us
    pallas_call x2, Pallas kernels, output(): pl.pallas_call(output_kernel, grid_spec=pltpu.PrefetchScalarGridSpec(num_...  18.9 us
  transfers between devices with their start and end apart: 19, of which 12 were waited for; matrix products, arithmetic and copies ran while one was open for 2% of the time, Pallas kernels for 11%

profile of v1, /device:TPU:0, one launch (start us, length us, event | category | flops | bytes accessed | tf_op | source)
XLA Modules:
  0.0 302.7 jit_solution(15239647029018982341)
XLA Ops:
  2.0 1.1 slice_bitcast_fusion.cache_ref
  3.1 1.5 shard_map.122
  5.5 132.4 %conditional.10 = (bf16[24,3072]{1,0:T(8,128)(2,1)S(1)}, bf16[24,3072]{1,0:T(8,128)(2,1)}, bf16[2,192,256]{2,1,0:T(8,128)(2,1)S(1)}, bf16[2,192,256]{2,1,0:T(8,1...) conditional(s32[]{:T(128)} %convert_element_type.13, ...), branch_computations={%region_0.1_spmd, %region_1.10_spmd} | conditional | flops 73729 | bytes 92799688 | solution.py:457
  5.5 2.0 collective-permute-start
  7.5 44.4 %conditional = (bf16[8,24,3072]{2,1,0:T(8,128)(2,1)}, bf16[2,192,256]{2,1,0:T(8,128)(2,1)S(1)}, bf16[192,512]{1,0:T(8,128)(2,1)S(1)}) conditional(s32[]{:T(128)} %convert_element_type.2, (f32[4,3072]{1,0:T(4,128)S(1)}, bf16[24,3072]{1,0:T(8,128)(2,1)S(1)}, bf16[8,24,3584]{2,1,0:T(8,128)(2,1)}) %tuple.63, (bf16[8,24,3584]{2,1,0:T(8,128)(2,1)}, ...), branch_computations={%region_2.2_spmd, %region_3.3_spmd} | conditional | bytes 4128824 | solution.py:372
  7.5 7.3 %all-to-all-start.1 = ((bf16[8,24,3584]{2,1,0:T(8,128)(2,1)}), bf16[8,24,3584]{2,1,0:T(8,128)(2,1)S(1)}, u32[]{:S(2)}, u32[]{:S(2)}) async-start(bf16[8,24,3584]{2,1,0:T(8,128)(2,1)} %get-tuple-element.234), calls=%async_computation.1 | async-start | bytes 2752512 | tf_op jit(solution)/shard_map/cond/branch_1_fun/cond/branch_1_fun/all_to_all | solution.py:280
  14.8 30.8 %all-to-all-done.1 = bf16[8,24,3584]{2,1,0:T(8,128)(2,1)S(1)} async-done(((bf16[8,24,3584]{2,1,0:T(8,128)(2,1)}), bf16[8,24,3584]{2,1,0:T(8,128)(2,1)S(1)}, u32[]{:S(2)}, u32[]{:S(2)}) %all-to-all-start.1) | async-done | bytes 1376288 | tf_op jit(solution)/shard_map/cond/branch_1_fun/cond/branch_1_fun/all_to_all | solution.py:280
  45.6 6.3 %branch_1_fun.22 = (bf16[192,3072]{1,0:T(8,128)(2,1)}, bf16[2,192,256]{2,1,0:T(8,128)(2,1)S(1)}) custom-call(f32[2,128]{1,0:T(2,128)S(1)} %get-tuple-element.231.gain_ref, bf16[3,3072,256]{2,1,0:T(8,128)(2,1)} %get-tuple-element.232.in_ref, bf16[1,256,3072]{2,1,0:T(8,128)(2,1)} %get-tuple-element.233.out_weights_ref, bf16[192,3584]{1,0:T(8,128)(2,1)S(1)} %bitcast.47, ...), custom_call_target="tpu_custom_call" | custom-call | tf_op jit(solution)/shard_map/cond/branch_1_fun/cond/branch_1_fun/pallas_call | solution.py:321
  51.9 3.8 %all-to-all-start.10 = ((bf16[8,24,3072]{2,1,0:T(8,128)(2,1)}), bf16[8,24,3072]{2,1,0:T(8,128)(2,1)S(1)}, u32[]{:S(2)}, u32[]{:S(2)}) async-start(bf16[8,24,3072]{2,1,0:T(8,128)(2,1)} %get-tuple-element.285), calls=%async_computation.10 | async-start | bytes 2359296 | tf_op jit(solution)/shard_map/cond/branch_1_fun/all_to_all | solution.py:280
  55.7 1.9 collective-permute-start.1
  57.6 2.4 collective-permute-start.2
  60.1 1.2 collective-permute-done.2
  61.3 12.3 %all-to-all-done.10 = bf16[8,24,3072]{2,1,0:T(8,128)(2,1)S(1)} async-done(((bf16[8,24,3072]{2,1,0:T(8,128)(2,1)}), bf16[8,24,3072]{2,1,0:T(8,128)(2,1)S(1)}, u32[]{:S(2)}, u32[]{:S(2)}) %all-to-all-start.10) | async-done | bytes 1179680 | tf_op jit(solution)/shard_map/cond/branch_1_fun/all_to_all | solution.py:280
  73.6 1.6 conditional.1
  73.6 1.6 branch_1_fun.24
  75.8 3.6 %all-to-all-start.11 = ((bf16[8,24,3072]{2,1,0:T(8,128)(2,1)}), bf16[8,24,3072]{2,1,0:T(8,128)(2,1)S(1)}, u32[]{:S(2)}, u32[]{:S(2)}) async-start(bf16[8,24,3072]{2,1,0:T(8,128)(2,1)} %get-tuple-element.291), calls=%async_computation.11 | async-start | bytes 2359296 | tf_op jit(solution)/shard_map/cond/branch_1_fun/all_to_all | solution.py:280
  79.4 1.9 collective-permute-start.3
  81.3 22.5 %all-to-all-done.11 = bf16[8,24,3072]{2,1,0:T(8,128)(2,1)S(1)} async-done(((bf16[8,24,3072]{2,1,0:T(8,128)(2,1)}), bf16[8,24,3072]{2,1,0:T(8,128)(2,1)S(1)}, u32[]{:S(2)}, u32[]{:S(2)}) %all-to-all-start.11) | async-done | bytes 1179680 | tf_op jit(solution)/shard_map/cond/branch_1_fun/all_to_all | solution.py:280
  104.6 7.2 %conditional.2 = (bf16[8,24,3072]{2,1,0:T(8,128)(2,1)}, bf16[2,192,256]{2,1,0:T(8,128)(2,1)}, bf16[24,3072]{1,0:T(8,128)(2,1)S(1)}) conditional(s32[]{:T(128)} %convert_element_type.2, (f32[4,3072]{1,0:T(4,128)S(1)}, f32[4,3072]{1,0:T(4,128)S(1)}, bf16[24,3072]{1,0:T(8,128)(2,1)S(1)}, bf16[8,24,3072]{2,1,0:T(8,128)(2,1)S(1)}, ...), branch_computations={%region_6.6_spmd, %region_7.7_spmd} | conditional | bytes 24 | solution.py:372
  104.6 7.2 %branch_1_fun.26 = (bf16[192,3072]{1,0:T(8,128)(2,1)}, bf16[2,192,256]{2,1,0:T(8,128)(2,1)}) custom-call(f32[2,128]{1,0:T(2,128)S(1)} %get-tuple-element.257.gain_ref, bf16[3,3072,256]{2,1,0:T(8,128)(2,1)} %get-tuple-element.258.in_ref, bf16[1,256,3072]{2,1,0:T(8,128)(2,1)} %get-tuple-element.259.out_weights_ref, bf16[192,3072]{1,0:T(8,128)(2,1)S(1)} %bitcast.59, ...), custom_call_target="tpu_custom_call" | custom-call | tf_op jit(solution)/shard_map/cond/branch_1_fun/cond/branch_1_fun/pallas_call | solution.py:321
  111.8 3.6 %all-to-all-start.12 = ((bf16[8,24,3072]{2,1,0:T(8,128)(2,1)}), bf16[8,24,3072]{2,1,0:T(8,128)(2,1)S(1)}, u32[]{:S(2)}, u32[]{:S(2)}) async-start(bf16[8,24,3072]{2,1,0:T(8,128)(2,1)} %get-tuple-element.296), calls=%async_computation.12 | async-start | bytes 2359296 | tf_op jit(solution)/shard_map/cond/branch_1_fun/all_to_all | solution.py:280
  115.4 2.1 collective-permute-start.4
  117.5 19.6 %all-to-all-done.12 = bf16[8,24,3072]{2,1,0:T(8,128)(2,1)S(1)} async-done(((bf16[8,24,3072]{2,1,0:T(8,128)(2,1)}), bf16[8,24,3072]{2,1,0:T(8,128)(2,1)S(1)}, u32[]{:S(2)}, u32[]{:S(2)}) %all-to-all-start.12) | async-done | bytes 1179680 | tf_op jit(solution)/shard_map/cond/branch_1_fun/all_to_all | solution.py:280
  138.0 23.0 %collective-permute-start.24 = (bf16[2048,3072]{1,0:T(8,128)(2,1)}, bf16[2048,3072]{1,0:T(8,128)(2,1)}, u32[]{:S(2)}, u32[]{:S(2)}) collective-permute-start(bf16[2048,3072]{1,0:T(8,128)(2,1)} %get-tuple-element.403), channel_id=1, source_target_pairs={{0,8},{1,9},{2,10},{3,11},{4,12},{5,13},{6,14},{7,15},{8,0},{9,1},... | collective-permute-start | bytes 37748744 | tf_op jit(solution)/shard_map/ppermute | solution.py:252
  161.5 5.4 %collective-permute-done.22 = bf16[24,3072]{1,0:T(8,128)(2,1)S(1)} collective-permute-done((bf16[24,3072]{1,0:T(8,128)(2,1)}, bf16[24,3072]{1,0:T(8,128)(2,1)S(1)}, u32[]{:S(2)}, u32[]{:S(2)}) %collective-permute-start.22) | collective-permute-done | bytes 147488 | tf_op jit(solution)/shard_map/ppermute | solution.py:260
  167.0 33.5 %conditional.11 = (bf16[8,24,3072]{2,1,0:T(8,128)(2,1)S(1)}) conditional(s32[]{:T(128)} %convert_element_type.12, () %tuple.100, (f32[4,3072]{1,0:T(4,128)S(1)}, bf16[24,3072]{1,0:T(8,128)(2,1)S(1)}) %tuple.99), branch_computations={%region_10.11_spmd, %region_11.12_spmd} | conditional | bytes 2359304 | solution.py:372
  167.0 1.9 branch_1_fun.34
  168.9 31.6 %all_to_all.66 = bf16[8,24,3072]{2,1,0:T(8,128)(2,1)S(1)} all-to-all(bf16[8,24,3072]{2,1,0:T(8,128)(2,1)S(1)} %branch_1_fun.34), channel_id=1, replica_groups=mesh['pipe'=4,'seq'=8] {'seq'}, dimensions={0} | all-to-all | bytes 2359296 | tf_op jit(solution)/shard_map/cond/branch_1_fun/all_to_all | solution.py:280
  200.5 16.8 %conditional.12 = (bf16[8,24,256]{2,1,0:T(8,128)(2,1)}, bf16[8,24,3072]{2,1,0:T(8,128)(2,1)S(1)}, bf16[2,192,256]{2,1,0:T(8,128)(2,1)S(1)}) conditional(s32[]{:T(128)} %convert_element_type.12, (f32[4,3072]{1,0:T(4,128)S(1)}, bf16[24,3072]{1,0:T(8,128)(2,1)S(1)}) %tuple.99, (bf16[8,24,3072]{2,1,0:T(8,128)(2,1)S(1)}, f32[2,128]{1,0:T(2,128)S(1)}, ...), branch_computations={%region_12.13_spmd, %region_13.14_spmd} | conditional | bytes 3539000 | solution.py:372
  200.5 5.6 %branch_1_fun.35 = (bf16[192,256]{1,0:T(8,128)(2,1)}, bf16[2,192,256]{2,1,0:T(8,128)(2,1)S(1)}) custom-call(f32[2,128]{1,0:T(2,128)S(1)} %get-tuple-element.304.gain_ref, bf16[3,3072,256]{2,1,0:T(8,128)(2,1)} %get-tuple-element.305.in_ref, bf16[1,256,3072]{2,1,0:T(8,128)(2,1)} %get-tuple-element.306.out_weights_ref, bf16[192,3072]{1,0:T(8,128)(2,1)S(1)} %bitcast.62, ...), custom_call_target="tpu_custom_call" | custom-call | tf_op jit(solution)/shard_map/cond/branch_1_fun/pallas_call | solution.py:321
  206.1 4.0 %all-to-all-start.5 = ((bf16[8,24,256]{2,1,0:T(8,128)(2,1)}), bf16[8,24,256]{2,1,0:T(8,128)(2,1)}, u32[]{:S(2)}, u32[]{:S(2)}) async-start(bf16[8,24,256]{2,1,0:T(8,128)(2,1)} %bitcast.12), calls=%async_computation.5 | async-start | bytes 196608 | tf_op jit(solution)/shard_map/cond/branch_1_fun/all_to_all | solution.py:280
  210.1 7.1 %all-to-all-done.5 = bf16[8,24,256]{2,1,0:T(8,128)(2,1)} async-done(((bf16[8,24,256]{2,1,0:T(8,128)(2,1)}), bf16[8,24,256]{2,1,0:T(8,128)(2,1)}, u32[]{:S(2)}, u32[]{:S(2)}) %all-to-all-start.5) | async-done | bytes 98336 | tf_op jit(solution)/shard_map/cond/branch_1_fun/all_to_all | solution.py:280
  218.7 32.2 %conditional.13 = (bf16[8,24,256]{2,1,0:T(8,128)(2,1)S(1)}, bf16[8,24,3072]{2,1,0:T(8,128)(2,1)}, bf16[2,192,256]{2,1,0:T(8,128)(2,1)S(1)}, bf16[24,3072]{1,0:T(8,128)(2,1)S(1)}) conditional(s32[]{:T(128)} %convert_element_type.12, (bf16[8,24,3072]{2,1,0:T(8,128)(2,1)S(1)}, f32[2,128]{1,0:T(2,128)S(1)}, bf16[3,3072,256]{2,1,0:T(8,128)(2,1)}, ...), branch_computations={%region_14.15_spmd, %region_15.16_spmd} | conditional | bytes 3539008 | solution.py:372
  218.7 10.1 %branch_1_fun.38 = (bf16[24,3072]{1,0:T(8,128)(2,1)S(1)}, bf16[8,24,3072]{2,1,0:T(8,128)(2,1)}) custom-call(s32[8]{0:T(128)S(1)} %get-tuple-element.318.order_ref, f32[4,3072]{1,0:T(4,128)S(1)} %get-tuple-element.319.params_ref, f32[4,3072]{1,0:T(4,128)S(1)} %get-tuple-element.320.next_ref, bf16[24,3072]{1,0:T(8,128)(2,1)S(1)} %get-tuple-element.321.x_ref, ...), custom_call_target="tpu_custom_call" | custom-call | tf_op jit(solution)/shard_map/cond/branch_1_fun/pallas_call | solution.py:344
  228.9 4.3 %all-to-all-start.7 = ((bf16[8,24,3072]{2,1,0:T(8,128)(2,1)}), bf16[8,24,3072]{2,1,0:T(8,128)(2,1)}, u32[]{:S(2)}, u32[]{:S(2)}) async-start(bf16[8,24,3072]{2,1,0:T(8,128)(2,1)} %get-tuple-element.324), calls=%async_computation.7 | async-start | bytes 2359296 | tf_op jit(solution)/shard_map/cond/branch_1_fun/all_to_all | solution.py:280
  233.1 17.8 %all-to-all-done.7 = bf16[8,24,3072]{2,1,0:T(8,128)(2,1)} async-done(((bf16[8,24,3072]{2,1,0:T(8,128)(2,1)}), bf16[8,24,3072]{2,1,0:T(8,128)(2,1)}, u32[]{:S(2)}, u32[]{:S(2)}) %all-to-all-start.7) | async-done | bytes 1179680 | tf_op jit(solution)/shard_map/cond/branch_1_fun/all_to_all | solution.py:280
  251.0 17.5 %conditional.14 = (bf16[8,24,256]{2,1,0:T(8,128)(2,1)}, bf16[8,24,3072]{2,1,0:T(8,128)(2,1)S(1)}, bf16[2,192,256]{2,1,0:T(8,128)(2,1)S(1)}, bf16[24,3072]{1,0:T(8,128)(2,1)S(1)}) conditional(s32[]{:T(128)} %convert_element_type.12, (s32[8]{0:T(128)S(1)}, f32[4,3072]{1,0:T(4,128)S(1)}, f32[4,3072]{1,0:T(4,128)S(1)}, ...), branch_computations={%region_16.17_spmd, %region_17.18_spmd} | conditional | bytes 3539008 | solution.py:372
  251.0 6.3 %branch_1_fun.40 = (bf16[192,256]{1,0:T(8,128)(2,1)}, bf16[2,192,256]{2,1,0:T(8,128)(2,1)S(1)}) custom-call(f32[2,128]{1,0:T(2,128)S(1)} %get-tuple-element.335.gain_ref, bf16[3,3072,256]{2,1,0:T(8,128)(2,1)} %get-tuple-element.336.in_ref, bf16[1,256,3072]{2,1,0:T(8,128)(2,1)} %get-tuple-element.337.out_weights_ref, bf16[192,3072]{1,0:T(8,128)(2,1)} %bitcast.15.blocks_ref, ...), custom_call_target="tpu_custom_call" | custom-call | tf_op jit(solution)/shard_map/cond/branch_1_fun/pallas_call | solution.py:321
  257.3 4.0 %all-to-all-start.9 = ((bf16[8,24,256]{2,1,0:T(8,128)(2,1)}), bf16[8,24,256]{2,1,0:T(8,128)(2,1)}, u32[]{:S(2)}, u32[]{:S(2)}) async-start(bf16[8,24,256]{2,1,0:T(8,128)(2,1)} %bitcast.16), calls=%async_computation.9 | async-start | bytes 196608 | tf_op jit(solution)/shard_map/cond/branch_1_fun/all_to_all | solution.py:280
  261.3 7.1 %all-to-all-done.9 = bf16[8,24,256]{2,1,0:T(8,128)(2,1)} async-done(((bf16[8,24,256]{2,1,0:T(8,128)(2,1)}), bf16[8,24,256]{2,1,0:T(8,128)(2,1)}, u32[]{:S(2)}, u32[]{:S(2)}) %all-to-all-start.9) | async-done | bytes 98336 | tf_op jit(solution)/shard_map/cond/branch_1_fun/all_to_all | solution.py:280
  268.4 1.4 collective-permute-done.25
  269.9 1.0 select_select_fusion
  270.9 14.5 %conditional.15 = (bf16[24,3072]{1,0:T(8,128)(2,1)S(1)}, bf16[8,24,1024]{2,1,0:T(8,128)(2,1)}) conditional(s32[]{:T(128)} %convert_element_type.12, (bf16[8,24,3072]{2,1,0:T(8,128)(2,1)S(1)}, f32[2,128]{1,0:T(2,128)S(1)}, bf16[3,3072,256]{2,1,0:T(8,128)(2,1)}, bf16[1,256,3072]{2,1,0:T(8,128)(2,1)}, bf16[2,192,256]{2,1,0:T(8,128)(2,1)S(1)}, ...), branch_computations={%region_18.19_spmd, %region_19.20_spmd} | conditional | flops 1572865 | bytes 3735578 | solution.py:372
  271.7 4.1 %all-to-all-start.15 = ((bf16[8,24,1024]{2,1,0:T(8,128)(2,1)}), bf16[8,24,1024]{2,1,0:T(8,128)(2,1)}, u32[]{:S(2)}, u32[]{:S(2)}) async-start(bf16[8,24,1024]{2,1,0:T(8,128)(2,1)} %pad_maximum_fusion.1), calls=%async_computation.15 | async-start | bytes 786432 | tf_op jit(solution)/shard_map/cond/branch_1_fun/all_to_all | solution.py:280
  275.8 8.8 %branch_1_fun.43 = bf16[24,3072]{1,0:T(8,128)(2,1)S(1)} custom-call(s32[8]{0:T(128)S(1)} %get-tuple-element.357.order_ref, f32[4,3072]{1,0:T(4,128)S(1)} %get-tuple-element.358.params_ref, f32[4,3072]{1,0:T(4,128)S(1)} %get-tuple-element.359.next_ref, bf16[24,3072]{1,0:T(8,128)(2,1)S(1)} %get-tuple-element.360.x_ref, ...), custom_call_target="tpu_custom_call" | custom-call | tf_op jit(solution)/shard_map/cond/branch_1_fun/pallas_call | solution.py:344
  285.4 1.0 select_select_fusion.2
  286.4 12.9 %collective-permute-start.26 = (bf16[24,3072]{1,0:T(8,128)(2,1)S(1)}, bf16[24,3072]{1,0:T(8,128)(2,1)S(1)}, u32[]{:S(2)}, u32[]{:S(2)}) collective-permute-start(bf16[24,3072]{1,0:T(8,128)(2,1)S(1)} %select_select_fusion.2), channel_id=1, source_target_pairs={{0,8},{1,9},{2,10},{3,11},{4,12},{5,13},{6,14},{7,15},{8,0},{9,1},... | collective-permute-start | bytes 442376 | tf_op jit(solution)/shard_map/ppermute | solution.py:252
  299.3 1.3 reshape.74
  (65 shorter events, 11.1 us)
Async XLA Ops:
  0.6 2.5 copy-start
  1.5 3.2 %collective-permute-start.21 = (f32[4,3072]{1,0:T(4,128)S(1)}, f32[4,3072]{1,0:T(4,128)S(1)}, u32[]{:S(2)}, u32[]{:S(2)}) collective-permute-start(f32[4,3072]{1,0:T(4,128)S(1)} %select_maximum_fusion.params_ref), channel_id=1, source_target_pairs={{0,8},{1,9},{2,10},{3,11},{4,12},{5,13},{6,14},{7,15},{8,0},{9,1},... | collective-permute-start | bytes 147464 | tf_op jit(solution)/shard_map/ppermute | solution.py:252
  5.5 155.4 %copy-start.9 = (s32[8]{0:T(128)S(1)}, s32[8]{0:T(128)}, u32[]{:S(2)}) copy-start(s32[8]{0:T(128)} %constant.55.clone) | copy-start | bytes 100
  5.5 68.0 %collective-permute-start = (bf16[3,3072,256]{2,1,0:T(8,128)(2,1)}, bf16[3,3072,256]{2,1,0:T(8,128)(2,1)}, u32[]{:S(2)}, u32[]{:S(2)}) collective-permute-start(bf16[3,3072,256]{2,1,0:T(8,128)(2,1)} %get-tuple-element.283), channel_id=1, source_target_pairs={{0,8},{1,9},{2,10},{3,11},{4,12},{5,13},{6,14},{7,15},{8,0},{9,1},... | collective-permute-start | bytes 14155784 | tf_op jit(solution)/shard_map/cond/branch_1_fun/ppermute | solution.py:252
  7.5 38.1 %all-to-all-start.1 = ((bf16[8,24,3584]{2,1,0:T(8,128)(2,1)}), bf16[8,24,3584]{2,1,0:T(8,128)(2,1)S(1)}, u32[]{:S(2)}, u32[]{:S(2)}) async-start(bf16[8,24,3584]{2,1,0:T(8,128)(2,1)} %get-tuple-element.234), calls=%async_computation.1 | async-start | bytes 2752512 | tf_op jit(solution)/shard_map/cond/branch_1_fun/cond/branch_1_fun/all_to_all | solution.py:280
  51.9 59.9 %copy-start.4 = (bf16[2,192,256]{2,1,0:T(8,128)(2,1)}, bf16[2,192,256]{2,1,0:T(8,128)(2,1)S(1)}, u32[]{:S(2)}) copy-start(bf16[2,192,256]{2,1,0:T(8,128)(2,1)S(1)} %get-tuple-element.468) | copy-start | bytes 589828 | tf_op jit(solution)/shard_map/cond
  51.9 21.6 %all-to-all-start.10 = ((bf16[8,24,3072]{2,1,0:T(8,128)(2,1)}), bf16[8,24,3072]{2,1,0:T(8,128)(2,1)S(1)}, u32[]{:S(2)}, u32[]{:S(2)}) async-start(bf16[8,24,3072]{2,1,0:T(8,128)(2,1)} %get-tuple-element.285), calls=%async_computation.10 | async-start | bytes 2359296 | tf_op jit(solution)/shard_map/cond/branch_1_fun/all_to_all | solution.py:280
  55.7 17.9 %collective-permute-start.1 = (bf16[1,256,3072]{2,1,0:T(8,128)(2,1)}, bf16[1,256,3072]{2,1,0:T(8,128)(2,1)}, u32[]{:S(2)}, u32[]{:S(2)}) collective-permute-start(bf16[1,256,3072]{2,1,0:T(8,128)(2,1)} %get-tuple-element.284), channel_id=1, source_target_pairs={{0,8},{1,9},{2,10},{3,11},{4,12},{5,13},{6,14},{7,15},{8,0},{9,1},... | collective-permute-start | bytes 4718600 | tf_op jit(solution)/shard_map/cond/branch_1_fun/ppermute | solution.py:252
  57.6 3.7 %collective-permute-start.2 = (bf16[2,192,256]{2,1,0:T(8,128)(2,1)S(1)}, bf16[2,192,256]{2,1,0:T(8,128)(2,1)S(1)}, u32[]{:S(2)}, u32[]{:S(2)}) collective-permute-start(bf16[2,192,256]{2,1,0:T(8,128)(2,1)S(1)} %get-tuple-element.468), channel_id=1, source_target_pairs={{0,8},{1,9},{2,10},{3,11},{4,12},{5,13},{6,14},{7,15},{8,0},{9,1},... | collective-permute-start | bytes 589832 | tf_op jit(solution)/shard_map/cond/branch_1_fun/ppermute | solution.py:252
  75.2 0.7 copy-start.7
  75.8 28.0 %all-to-all-start.11 = ((bf16[8,24,3072]{2,1,0:T(8,128)(2,1)}), bf16[8,24,3072]{2,1,0:T(8,128)(2,1)S(1)}, u32[]{:S(2)}, u32[]{:S(2)}) async-start(bf16[8,24,3072]{2,1,0:T(8,128)(2,1)} %get-tuple-element.291), calls=%async_computation.11 | async-start | bytes 2359296 | tf_op jit(solution)/shard_map/cond/branch_1_fun/all_to_all | solution.py:280
  79.4 24.5 %collective-permute-start.3 = (bf16[192,512]{1,0:T(8,128)(2,1)S(1)}, bf16[192,512]{1,0:T(8,128)(2,1)S(1)}, u32[]{:S(2)}, u32[]{:S(2)}) collective-permute-start(bf16[192,512]{1,0:T(8,128)(2,1)S(1)} %get-tuple-element.294), channel_id=1, source_target_pairs={{0,8},{1,9},{2,10},{3,11},{4,12},{5,13},{6,14},{7,15},{8,0},{9,1},... | collective-permute-start | bytes 589832 | tf_op jit(solution)/shard_map/cond/branch_1_fun/ppermute | solution.py:252
  103.9 0.7 copy-start.6
  104.5 32.5 %copy-start.3 = (bf16[1,256,3072]{2,1,0:T(8,128)(2,1)S(1)}, bf16[1,256,3072]{2,1,0:T(8,128)(2,1)}, u32[]{:S(2)}) copy-start(bf16[1,256,3072]{2,1,0:T(8,128)(2,1)} %get-tuple-element.284) | copy-start | bytes 4718596 | tf_op jit(solution)/shard_map/cond
  111.8 25.3 %all-to-all-start.12 = ((bf16[8,24,3072]{2,1,0:T(8,128)(2,1)}), bf16[8,24,3072]{2,1,0:T(8,128)(2,1)S(1)}, u32[]{:S(2)}, u32[]{:S(2)}) async-start(bf16[8,24,3072]{2,1,0:T(8,128)(2,1)} %get-tuple-element.296), calls=%async_computation.12 | async-start | bytes 2359296 | tf_op jit(solution)/shard_map/cond/branch_1_fun/all_to_all | solution.py:280
  115.4 22.5 %copy-start.5 = (bf16[2,192,256]{2,1,0:T(8,128)(2,1)S(1)}, bf16[2,192,256]{2,1,0:T(8,128)(2,1)}, u32[]{:S(2)}) copy-start(bf16[2,192,256]{2,1,0:T(8,128)(2,1)} %copy-done.4) | copy-start | bytes 589828 | tf_op jit(solution)/shard_map/cond
  115.4 21.6 %collective-permute-start.4 = (bf16[2,192,256]{2,1,0:T(8,128)(2,1)}, bf16[2,192,256]{2,1,0:T(8,128)(2,1)}, u32[]{:S(2)}, u32[]{:S(2)}) collective-permute-start(bf16[2,192,256]{2,1,0:T(8,128)(2,1)} %get-tuple-element.297), channel_id=1, source_target_pairs={{0,8},{1,9},{2,10},{3,11},{4,12},{5,13},{6,14},{7,15},{8,0},{9,1},... | collective-permute-start | bytes 589832 | tf_op jit(solution)/shard_map/cond/branch_1_fun/ppermute | solution.py:252
  137.9 79.3 %copy-start.8 = (s32[8]{0:T(128)S(1)}, s32[8]{0:T(128)}, u32[]{:S(2)}) copy-start(s32[8]{0:T(128)} %constant.57.clone) | copy-start | bytes 100
  137.9 80.0 %copy-start.2 = (s32[8]{0:T(128)S(1)}, s32[8]{0:T(128)}, u32[]{:S(2)}) copy-start(s32[8]{0:T(128)} %constant.56.clone) | copy-start | bytes 100
  138.0 113.0 %collective-permute-start.24 = (bf16[2048,3072]{1,0:T(8,128)(2,1)}, bf16[2048,3072]{1,0:T(8,128)(2,1)}, u32[]{:S(2)}, u32[]{:S(2)}) collective-permute-start(bf16[2048,3072]{1,0:T(8,128)(2,1)} %get-tuple-element.403), channel_id=1, source_target_pairs={{0,8},{1,9},{2,10},{3,11},{4,12},{5,13},{6,14},{7,15},{8,0},{9,1},... | collective-permute-start | bytes 37748744 | tf_op jit(solution)/shard_map/ppermute | solution.py:252
  160.9 6.0 %collective-permute-start.22 = (bf16[24,3072]{1,0:T(8,128)(2,1)}, bf16[24,3072]{1,0:T(8,128)(2,1)S(1)}, u32[]{:S(2)}, u32[]{:S(2)}) collective-permute-start(bf16[24,3072]{1,0:T(8,128)(2,1)} %get-tuple-element.397), channel_id=1, source_target_pairs={{0,16},{1,17},{2,18},{3,19},{4,20},{5,21},{6,22},{7,23},{8,24},{9,... | collective-permute-start | bytes 442376 | tf_op jit(solution)/shard_map/ppermute | solution.py:260
  206.1 11.2 %all-to-all-start.5 = ((bf16[8,24,256]{2,1,0:T(8,128)(2,1)}), bf16[8,24,256]{2,1,0:T(8,128)(2,1)}, u32[]{:S(2)}, u32[]{:S(2)}) async-start(bf16[8,24,256]{2,1,0:T(8,128)(2,1)} %bitcast.12), calls=%async_computation.5 | async-start | bytes 196608 | tf_op jit(solution)/shard_map/cond/branch_1_fun/all_to_all | solution.py:280
  217.3 1.4 collective-permute-start.23
  228.9 22.1 %all-to-all-start.7 = ((bf16[8,24,3072]{2,1,0:T(8,128)(2,1)}), bf16[8,24,3072]{2,1,0:T(8,128)(2,1)}, u32[]{:S(2)}, u32[]{:S(2)}) async-start(bf16[8,24,3072]{2,1,0:T(8,128)(2,1)} %get-tuple-element.324), calls=%async_computation.7 | async-start | bytes 2359296 | tf_op jit(solution)/shard_map/cond/branch_1_fun/all_to_all | solution.py:280
  257.3 11.2 %all-to-all-start.9 = ((bf16[8,24,256]{2,1,0:T(8,128)(2,1)}), bf16[8,24,256]{2,1,0:T(8,128)(2,1)}, u32[]{:S(2)}, u32[]{:S(2)}) async-start(bf16[8,24,256]{2,1,0:T(8,128)(2,1)} %bitcast.16), calls=%async_computation.9 | async-start | bytes 196608 | tf_op jit(solution)/shard_map/cond/branch_1_fun/all_to_all | solution.py:280
  268.4 1.4 collective-permute-start.25
  271.7 13.7 %all-to-all-start.15 = ((bf16[8,24,1024]{2,1,0:T(8,128)(2,1)}), bf16[8,24,1024]{2,1,0:T(8,128)(2,1)}, u32[]{:S(2)}, u32[]{:S(2)}) async-start(bf16[8,24,1024]{2,1,0:T(8,128)(2,1)} %pad_maximum_fusion.1), calls=%async_computation.15 | async-start | bytes 786432 | tf_op jit(solution)/shard_map/cond/branch_1_fun/all_to_all | solution.py:280
  285.4 17.3 %copy-start.1 = (bf16[2,24,3072]{2,1,0:T(8,128)(2,1)S(1)}, bf16[2,24,3072]{2,1,0:T(8,128)(2,1)}, u32[]{:S(2)}) copy-start(bf16[2,24,3072]{2,1,0:T(8,128)(2,1)} %param.31) | copy-start | bytes 884740
  286.4 15.5 %collective-permute-start.26 = (bf16[24,3072]{1,0:T(8,128)(2,1)S(1)}, bf16[24,3072]{1,0:T(8,128)(2,1)S(1)}, u32[]{:S(2)}, u32[]{:S(2)}) collective-permute-start(bf16[24,3072]{1,0:T(8,128)(2,1)S(1)} %select_select_fusion.2), channel_id=1, source_target_pairs={{0,8},{1,9},{2,10},{3,11},{4,12},{5,13},{6,14},{7,15},{8,0},{9,1},... | collective-permute-start | bytes 442376 | tf_op jit(solution)/shard_map/ppermute | solution.py:252
